TPU v7x, 32 devices: a whole 2x2x4 slice. The times are simulated.
32 devices in a mesh: gx: 4 (over z), gy: 8 (over y, x, core).
Axes of the slice: x: 2, y: 2, z: 4, core: 2. Of those that a mesh axis runs over, the one named last changes fastest.
Arguments:
- source_term: float32 [512, 125], P(('gx', 'gy')), may hold values from -24 to 24
- pressure_prev: float32 [512, 125], P(('gx', 'gy')), may hold values from -6 to 6
- diag_blocks: float32 [512, 125, 125], P(('gx', 'gy')), as said below
- local_neighbour: int32 [512, 4], P(('gx', 'gy')), may hold values from 0 to 15
- local_blocks: bfloat16 [512, 4, 125, 125], P(('gx', 'gy')), may hold values from -0.5 to 0.5
- send_element: int32 [4, 8, 8, 3], P('gx', 'gy'), may hold values from 0 to 15
- send_count: int32 [4, 8, 8], P('gx', 'gy'), may hold values from 1 to 3
- send_blocks: bfloat16 [4, 8, 8, 3, 125, 125], P('gx', 'gy'), may hold values from -0.5 to 0.5
- receive_element: int32 [4, 8, 8, 3], P('gx', 'gy'), may hold values from 0 to 15
- layer_count: int32 [128], P(('gx', 'gy')), may hold values from 1 to 4
Outputs:
- pressure: float32 [512, 125], P(('gx', 'gy'))
Inputs may be any that keep to these rules, and one draw needn't show every extreme that they name: `diag_blocks`: every block is nonsingular.
All inputs are finite; a program needn't handle non-finite values.
Results may differ from a plain program's by a relative error of at most 0.0003.
Values may be sent and summed in bfloat16 or wider, within the bound.
A program may use at most 64 MiB of HBM per device.

v0:
```python
import functools

import jax
import jax.numpy as jnp
from jax import lax
from jax.experimental import pallas as pl
from jax.experimental.pallas import tpu as pltpu
from jax.sharding import PartitionSpec as P

LAYERS = 4
NS_ITERS = 8
SWEEPS = 3
RELAXATION = 0.8
OFFSETS = ((-1, -1), (-1, 0), (-1, 1), (0, -1), (0, 1), (1, -1), (1, 0), (1, 1))
MESH = pl.DeviceIdType.MESH
BF16 = jnp.bfloat16
F32 = jnp.float32
W = 128
GROUP = 16
CHUNK = 4


def dot(a, b):
    return jnp.dot(a, b, preferred_element_type=F32)


def split(x):
    hi = x.astype(BF16)
    return hi, (x - hi.astype(F32)).astype(BF16)


def padded(x, rows):
    return jnp.pad(x, ((0, rows - x.shape[0]), (0, W - x.shape[1])))


def kernel(
    source_ref,
    prev_ref,
    diag_hbm,
    near_ref,
    local_hbm,
    send_el_ref,
    count_ref,
    send_hbm,
    recv_el_ref,
    layer_ref,
    out_ref,
    diag_in,
    local_in,
    send_in,
    fx_f,
    fx_s,
    blocks,
    sends,
    sendbuf,
    recvbuf,
    load_sem,
    send_sem,
    recv_sem,
):
    elements, width = source_ref.shape
    faces = near_ref.shape[1]
    slots = send_el_ref.shape[3]
    nx, ny = lax.axis_size("gx"), lax.axis_size("gy")
    gx, gy = lax.axis_index("gx"), lax.axis_index("gy")

    def there(k):
        a, b = OFFSETS[k]
        x, y = gx + a, gy + b
        return (x >= 0) & (x < nx) & (y >= 0) & (y < ny), (x, y)

    load_send = pltpu.make_async_copy(send_hbm.at[0, 0], send_in, load_sem.at[0])
    load_diag = pltpu.make_async_copy(diag_hbm, diag_in, load_sem.at[1])
    load_local = pltpu.make_async_copy(local_hbm, local_in, load_sem.at[2])
    load_send.start()
    load_diag.start()
    load_local.start()

    barrier = pltpu.get_barrier_semaphore()
    present = jnp.int32(0)
    for k in range(8):
        exists, target = there(k)
        present = present + exists.astype(jnp.int32)

        @pl.when(exists)
        def _():
            pl.semaphore_signal(barrier, inc=1, device_id=target, device_id_type=MESH)

        @pl.when(jnp.logical_not(exists))
        def _():
            for t in range(SWEEPS):
                recvbuf[t, k] = jnp.zeros((8, W), F32)

    lane = lax.broadcasted_iota(jnp.int32, (W, W), 1)
    lane_row = lax.broadcasted_iota(jnp.int32, (1, W), 1)
    element = lane % GROUP
    group = lane // GROUP

    index = jnp.full((1, W), -1, jnp.int32)
    for f in range(faces):
        for e in range(elements):
            index = jnp.where(lane_row == f * GROUP + e, near_ref[e, f], index)
    for k in range(8):
        count = count_ref[0, 0, k]
        for s in range(slots):
            chosen = jnp.where(s < count, send_el_ref[0, 0, k, s], -1)
            index = jnp.where(lane_row == 64 + 8 * k + s, chosen, index)
    select = (lax.broadcasted_iota(jnp.int32, (W, W), 0) == index).astype(F32).astype(BF16)
    row8 = lax.broadcasted_iota(jnp.int32, (8, W), 0)
    scatter_rows = []
    for k in range(8):
        target_el = jnp.full((8, W), -1, jnp.int32)
        for s in range(slots):
            target_el = jnp.where(row8 == s, recv_el_ref[0, 0, k, s], target_el)
        scatter_rows.append(target_el)
    scatter = jnp.concatenate(scatter_rows, axis=0)
    scatter = (scatter == lax.broadcasted_iota(jnp.int32, (64, W), 1) % GROUP).astype(F32).astype(BF16)

    depth = jnp.zeros((1, W), jnp.int32)
    for c in range(elements // LAYERS):
        depth = jnp.where((lane_row % GROUP) // LAYERS == c, layer_ref[c], depth)
    alive = (lane_row % LAYERS < depth).astype(F32)

    def nodes_first(x):
        rows = padded(x, elements)
        return jnp.concatenate([rows] * (W // GROUP), axis=0).T

    source = nodes_first(source_ref[...])
    pressure = nodes_first(prev_ref[...]) * alive

    def gathered(p):
        return dot(p.astype(BF16), select)

    def send_part(t, g):
        zero = jnp.zeros_like(g)
        low = jnp.where((lane >= 64) & (lane < 96), g, zero)
        high = jnp.where(lane >= 96, g, zero)
        rhs = jnp.concatenate([low, high], axis=0).astype(BF16)
        acc = zero
        for k in range(4):
            res = dot(sends[k].reshape(slots * W, 2 * W), rhs)
            for s in range(slots):
                acc = jnp.where((lane >= 64) & (lane % 32 == 8 * k + s), res[s * W : (s + 1) * W], acc)
        sendbuf[t] = acc.T[64:].reshape(8, 8, W)
        for k in range(8):
            exists, target = there(k)

            @pl.when(exists)
            def _():
                remote(t, k, 7 - k, target).start()

    def remote(t, k, landing, target):
        return pltpu.make_async_remote_copy(
            src_ref=sendbuf.at[t, k],
            dst_ref=recvbuf.at[t, landing],
            send_sem=send_sem.at[t, k],
            recv_sem=recv_sem.at[t, landing],
            device_id=target,
            device_id_type=MESH,
        )

    load_send.wait()

    for k in range(4):

        def prepare_send(s, carry, k=k):
            for half in range(2):
                sends[k, s, :, half * W : (half + 1) * W] = padded(send_in[k + 4 * half, s], W)
            return carry

        lax.fori_loop(0, slots, prepare_send, 0)
    pl.semaphore_wait(barrier, present)
    g = gathered(pressure)
    send_part(0, g)

    load_diag.wait()

    def doubled(x):
        return jnp.concatenate([x, x], axis=0)

    def store_split(e, start, x):
        hi, lo = split(x)
        rows = x.shape[0]
        fx_s[e, start : start + rows, 0:W] = hi
        fx_s[e, start : start + rows, W : 2 * W] = lo

    def prepare_diag(i, carry):
        for u in range(CHUNK):
            e = i * CHUNK + u
            m = padded(diag_in[e], W)
            magnitude = jnp.abs(m)
            column_norm = jnp.max(jnp.sum(magnitude, axis=0, keepdims=True), axis=1, keepdims=True)
            row_norm = jnp.max(jnp.sum(magnitude, axis=1, keepdims=True), axis=0, keepdims=True)
            x = m.T * (1.0 / (column_norm * row_norm))
            hi, lo = split(m)
            blocks[e, :, 4 * W : 5 * W] = hi
            blocks[e, :, 5 * W : 6 * W] = lo
            fx_f[e, W:] = x
            store_split(e, W, x)
            res = dot(blocks[e, :, 4 * W :], doubled(fx_s[e, W:]))
            f = res[:, :W] + res[:, W:]
            fx_f[e, :W] = f
            store_split(e, 0, f)
        return carry

    lax.fori_loop(0, elements // CHUNK, prepare_diag, 0)

    def step(k, carry):
        for e in range(elements):
            both = fx_s[e]
            res = dot(both, doubled(both[:W]))
            new = 2.0 * fx_f[e] - (res[:, :W] + res[:, W:])
            fx_f[e] = new
            store_split(e, 0, new)
        return carry

    lax.fori_loop(0, NS_ITERS - 1, step, 0)
    for e in range(elements):
        res = dot(fx_s[e, W:], doubled(fx_s[e, :W]))
        store_split(e, W, 2.0 * fx_f[e, W:] - (res[:, :W] + res[:, W:]))

    load_local.wait()

    def prepare_local(e, carry):
        for f in range(faces):
            blocks[e, :, f * W : (f + 1) * W] = padded(local_in[e, f], W)
        return carry

    lax.fori_loop(0, elements, prepare_local, 0)

    def per_element(load, rhs):
        acc = jnp.zeros((W, W), F32)
        for i in range(elements // CHUNK):
            res = dot(load(i * CHUNK), rhs)
            for u in range(CHUNK):
                acc = jnp.where(element == i * CHUNK + u, res[u * W : (u + 1) * W], acc)
        return acc

    for t in range(SWEEPS):
        zero = jnp.zeros_like(g)
        hi, lo = split(pressure)
        near = [jnp.where(group == f, g, zero).astype(BF16) for f in range(faces)]
        own = jnp.where(group == 4, hi.astype(F32), jnp.where(group == 5, lo.astype(F32), zero)).astype(BF16)
        acc = per_element(
            lambda e: blocks[e : e + CHUNK].reshape(CHUNK * W, 6 * W),
            jnp.concatenate(near + [own, own], axis=0),
        )
        for shift in (64, 32, 16):
            acc = acc + pltpu.roll(acc, shift, 1)
        local = source - acc

        for k in range(8):
            exists, target = there(k)

            @pl.when(exists)
            def _():
                remote(t, k, k, target).wait_recv()

        arrived = recvbuf[t].reshape(64, W).T
        arrived_hi, arrived_lo = split(arrived)
        residual = local - (dot(arrived_hi, scatter) + dot(arrived_lo, scatter))
        hi, lo = split(residual)
        rhs = jnp.where(group % 2 == 0, hi.astype(F32), lo.astype(F32)).astype(BF16)
        acc = per_element(
            lambda e: fx_s[e : e + CHUNK, W:].reshape(CHUNK * W, 2 * W), doubled(rhs)
        )
        acc = acc + pltpu.roll(acc, 16, 1)
        pressure = pressure + RELAXATION * alive * acc
        if t + 1 < SWEEPS:
            g = gathered(pressure)
            send_part(t + 1, g)

    out_ref[...] = pressure.T[:elements, :width]

    for t in range(SWEEPS):
        for k in range(8):
            exists, target = there(k)

            @pl.when(exists)
            def _():
                remote(t, k, k, target).wait_send()


def on_device(*args):
    source, prev, diag, near, local, send_el, count, send, recv_el, layers = args
    elements, width = source.shape
    faces = near.shape[1]
    slots = send_el.shape[3]
    vmem = pl.BlockSpec(memory_space=pltpu.VMEM)
    smem = pl.BlockSpec(memory_space=pltpu.SMEM)
    hbm = pl.BlockSpec(memory_space=pl.ANY)
    return pl.pallas_call(
        kernel,
        out_shape=jax.ShapeDtypeStruct(source.shape, F32),
        in_specs=[vmem, vmem, hbm, smem, hbm, smem, smem, hbm, smem, smem],
        out_specs=vmem,
        scratch_shapes=[
            pltpu.VMEM(diag.shape, F32),
            pltpu.VMEM(local.shape, BF16),
            pltpu.VMEM(send.shape[2:], BF16),
            pltpu.VMEM((elements, 2 * W, W), F32),
            pltpu.VMEM((elements, 2 * W, 2 * W), BF16),
            pltpu.VMEM((elements, W, 6 * W), BF16),
            pltpu.VMEM((4, slots, W, 2 * W), BF16),
            pltpu.VMEM((SWEEPS, 8, 8, W), F32),
            pltpu.VMEM((SWEEPS, 8, 8, W), F32),
            pltpu.SemaphoreType.DMA((3,)),
            pltpu.SemaphoreType.DMA((SWEEPS, 8)),
            pltpu.SemaphoreType.DMA((SWEEPS, 8)),
        ],
        compiler_params=pltpu.CompilerParams(
            collective_id=0, has_side_effects=True, vmem_limit_bytes=48 * 1024 * 1024
        ),
    )(*args)


def solution(mesh):
    return jax.shard_map(
        on_device,
        mesh=mesh,
        in_specs=(
            P(("gx", "gy"), None),
            P(("gx", "gy"), None),
            P(("gx", "gy"), None, None),
            P(("gx", "gy"), None),
            P(("gx", "gy"), None, None, None),
            P("gx", "gy", None, None),
            P("gx", "gy", None),
            P("gx", "gy", None, None, None, None),
            P("gx", "gy", None, None),
            P(("gx", "gy")),
        ),
        out_specs=P(("gx", "gy"), None),
        check_vma=False,
    )
```

profile of v0, /device:TPU:1, one launch (start us, length us, event | category | flops | bytes accessed | tf_op | source)
XLA Modules:
  0.0 31.3 jit_solution(1123527079815336218)
XLA Ops:
  0.0 0.0 copy-start.4
  0.0 0.9 %copy.14.send_el_ref = s32[1,1,8,3]{3,2,1,0:T(8,128)S(1)} copy(s32[1,1,8,3]{2,1,3,0:T(1,128)} %param.15) | data formatting | bytes 192 | tf_op args[5]
  0.9 0.8 %copy.16.recv_el_ref = s32[1,1,8,3]{3,2,1,0:T(8,128)S(1)} copy(s32[1,1,8,3]{2,1,3,0:T(1,128)} %param.18) | data formatting | bytes 192 | tf_op args[8]
  1.7 0.8 %copy.12.near_ref = s32[16,4]{1,0:T(8,128)S(1)} copy(s32[16,4]{0,1:T(4,128)} %param.13) | data formatting | bytes 512 | tf_op args[3]
  2.4 1.3 %copy.15.send_hbm = bf16[1,1,8,3,125,125]{5,4,3,2,1,0:T(8,128)(2,1)S(1)} copy(bf16[1,1,8,3,125,125]{5,2,4,3,1,0:T(8,128)(2,1)} %param.17) | data formatting | bytes 1500000 | tf_op args[7]
  3.7 1.6 %copy.11.diag_hbm = f32[16,125,125]{2,1,0:T(8,128)S(1)} copy(f32[16,125,125]{2,0,1:T(8,128)} %param.12) | data formatting | bytes 2000000 | tf_op args[2]
  5.3 0.0 copy-done.4
  5.3 0.0 copy-start
  5.3 0.0 copy-start.1
  5.3 0.0 copy-start.2
  5.3 0.0 copy-start.3
  5.3 0.5 %copy.13.local_hbm = bf16[16,4,125,125]{3,2,1,0:T(8,128)(2,1)S(1)} copy(bf16[16,4,125,125]{3,1,2,0:T(4,128)(2,1)S(1)} %copy-done.4) | data formatting | bytes 4000000 | tf_op args[4]
  5.9 0.1 copy-done
  6.0 0.0 copy-done.1
  6.0 0.0 copy-done.2
  6.0 0.0 copy-done.3
  6.0 24.6 %shard_map.100 = f32[16,125]{1,0:T(8,128)S(1)} custom-call(f32[16,125]{1,0:T(8,128)S(1)} %copy-done, f32[16,125]{1,0:T(8,128)S(1)} %copy-done.1, f32[16,125,125]{2,1,0:T(8,128)S(1)} %copy.11.diag_hbm, s32[16,4]{1,0:T(8,128)S(1)} %copy.12.near_ref, bf16[16,4,125,125]{3,2,1,0:T(8,128)(2,1)S(1)} %copy.13.local_hbm, s32[1,1,8,3]{3,2,1,0:T(8,128)S(1)} %copy.14.send_el_ref, ...), custom_call_target="tpu_custom_call" | custom-call | tf_op jit(solution)/shard_map/pallas_call | solution.py:292
  30.7 0.6 %copy.18 = f32[16,125]{1,0:T(8,128)} copy(f32[16,125]{1,0:T(8,128)S(1)} %shard_map.100) | data formatting | bytes 16000
Async XLA Ops:
  0.0 5.3 %copy-start.4 = (bf16[16,4,125,125]{3,1,2,0:T(4,128)(2,1)S(1)}, bf16[16,4,125,125]{3,1,2,0:T(4,128)(2,1)}, u32[]{:S(2)}) copy-start(bf16[16,4,125,125]{3,1,2,0:T(4,128)(2,1)} %param.14) | copy-start | bytes 6000004
  5.3 0.7 %copy-start = (f32[16,125]{1,0:T(8,128)S(1)}, f32[16,125]{1,0:T(8,128)}, u32[]{:S(2)}) copy-start(f32[16,125]{1,0:T(8,128)} %source_ref.1) | copy-start | bytes 24004
  5.3 0.7 %copy-start.1 = (f32[16,125]{1,0:T(8,128)S(1)}, f32[16,125]{1,0:T(8,128)}, u32[]{:S(2)}) copy-start(f32[16,125]{1,0:T(8,128)} %prev_ref.1) | copy-start | bytes 24004
  5.3 0.7 %copy-start.2 = (s32[1,1,8]{2,1,0:T(1,128)S(1)}, s32[1,1,8]{2,1,0:T(1,128)}, u32[]{:S(2)}) copy-start(s32[1,1,8]{2,1,0:T(1,128)} %count_ref.1) | copy-start | bytes 100
  5.3 0.7 %copy-start.3 = (s32[4]{0:T(128)S(1)}, s32[4]{0:T(128)}, u32[]{:S(2)}) copy-start(s32[4]{0:T(128)} %layer_ref.1) | copy-start | bytes 52
where the time goes:
time: 31.6 us; the launch traced here: 31.3 us
  Pallas kernels  24.6 us (78%)
  local copies, waits for them, and re-layouts  6.54 us (21%)
    pallas_call x1, Pallas kernels, on_device(): pl.pallas_call(kernel, out_shape=jax.ShapeDtypeStruct(source.shape, F32),...  24.6 us
    unnamed x17, local copies, waits for them, and re-layouts  6.54 us

commit v1 on v0

--- a/solution.py
+++ b/solution.py
@@ -36,31 +36,28 @@
 def kernel(
     source_ref,
     prev_ref,
-    diag_hbm,
+    diag_in,
     near_ref,
-    local_hbm,
+    local_in,
     send_el_ref,
     count_ref,
-    send_hbm,
+    send_in,
     recv_el_ref,
     layer_ref,
     out_ref,
-    diag_in,
-    local_in,
-    send_in,
+    send_wide,
     fx_f,
     fx_s,
     blocks,
     sends,
     sendbuf,
     recvbuf,
-    load_sem,
     send_sem,
     recv_sem,
 ):
     elements, width = source_ref.shape
-    faces = near_ref.shape[1]
-    slots = send_el_ref.shape[3]
+    faces = near_ref.shape[0]
+    slots = send_el_ref.shape[0]
     nx, ny = lax.axis_size("gx"), lax.axis_size("gy")
     gx, gy = lax.axis_index("gx"), lax.axis_index("gy")
 
@@ -68,13 +65,6 @@
         a, b = OFFSETS[k]
         x, y = gx + a, gy + b
         return (x >= 0) & (x < nx) & (y >= 0) & (y < ny), (x, y)
-
-    load_send = pltpu.make_async_copy(send_hbm.at[0, 0], send_in, load_sem.at[0])
-    load_diag = pltpu.make_async_copy(diag_hbm, diag_in, load_sem.at[1])
-    load_local = pltpu.make_async_copy(local_hbm, local_in, load_sem.at[2])
-    load_send.start()
-    load_diag.start()
-    load_local.start()
 
     barrier = pltpu.get_barrier_semaphore()
     present = jnp.int32(0)
@@ -99,11 +89,11 @@
     index = jnp.full((1, W), -1, jnp.int32)
     for f in range(faces):
         for e in range(elements):
-            index = jnp.where(lane_row == f * GROUP + e, near_ref[e, f], index)
+            index = jnp.where(lane_row == f * GROUP + e, near_ref[f, e], index)
     for k in range(8):
         count = count_ref[0, 0, k]
         for s in range(slots):
-            chosen = jnp.where(s < count, send_el_ref[0, 0, k, s], -1)
+            chosen = jnp.where(s < count, send_el_ref[s, 0, k], -1)
             index = jnp.where(lane_row == 64 + 8 * k + s, chosen, index)
     select = (lax.broadcasted_iota(jnp.int32, (W, W), 0) == index).astype(F32).astype(BF16)
     row8 = lax.broadcasted_iota(jnp.int32, (8, W), 0)
@@ -111,7 +101,7 @@
     for k in range(8):
         target_el = jnp.full((8, W), -1, jnp.int32)
         for s in range(slots):
-            target_el = jnp.where(row8 == s, recv_el_ref[0, 0, k, s], target_el)
+            target_el = jnp.where(row8 == s, recv_el_ref[s, 0, k], target_el)
         scatter_rows.append(target_el)
     scatter = jnp.concatenate(scatter_rows, axis=0)
     scatter = (scatter == lax.broadcasted_iota(jnp.int32, (64, W), 1) % GROUP).astype(F32).astype(BF16)
@@ -159,21 +149,16 @@
             device_id_type=MESH,
         )
 
-    load_send.wait()
-
+    send_wide[...] = send_in[...].astype(F32)
     for k in range(4):
-
-        def prepare_send(s, carry, k=k):
+        for s in range(slots):
             for half in range(2):
-                sends[k, s, :, half * W : (half + 1) * W] = padded(send_in[k + 4 * half, s], W)
-            return carry
-
-        lax.fori_loop(0, slots, prepare_send, 0)
+                rows = pl.ds(s * width * 8 + k + 4 * half, width, stride=8)
+                block = padded(send_wide[rows, :], W).astype(BF16)
+                sends[k, s, :, half * W : (half + 1) * W] = block
     pl.semaphore_wait(barrier, present)
     g = gathered(pressure)
     send_part(0, g)
-
-    load_diag.wait()
 
     def doubled(x):
         return jnp.concatenate([x, x], axis=0)
@@ -187,7 +172,7 @@
     def prepare_diag(i, carry):
         for u in range(CHUNK):
             e = i * CHUNK + u
-            m = padded(diag_in[e], W)
+            m = padded(diag_in[pl.ds(e, width, stride=elements), :], W)
             magnitude = jnp.abs(m)
             column_norm = jnp.max(jnp.sum(magnitude, axis=0, keepdims=True), axis=1, keepdims=True)
             row_norm = jnp.max(jnp.sum(magnitude, axis=1, keepdims=True), axis=0, keepdims=True)
@@ -219,8 +204,6 @@
         res = dot(fx_s[e, W:], doubled(fx_s[e, :W]))
         store_split(e, W, 2.0 * fx_f[e, W:] - (res[:, :W] + res[:, W:]))
 
-    load_local.wait()
-
     def prepare_local(e, carry):
         for f in range(faces):
             blocks[e, :, f * W : (f + 1) * W] = padded(local_in[e, f], W)
@@ -286,32 +269,33 @@
     elements, width = source.shape
     faces = near.shape[1]
     slots = send_el.shape[3]
+    diag = diag.transpose(1, 0, 2).reshape(width * elements, width)
+    send = send[0, 0].transpose(1, 2, 0, 3).reshape(slots * width * 8, width)
+    near = near.T
+    send_el = send_el.transpose(3, 0, 1, 2).reshape(slots, 1, 8)
+    recv_el = recv_el.transpose(3, 0, 1, 2).reshape(slots, 1, 8)
     vmem = pl.BlockSpec(memory_space=pltpu.VMEM)
     smem = pl.BlockSpec(memory_space=pltpu.SMEM)
-    hbm = pl.BlockSpec(memory_space=pl.ANY)
     return pl.pallas_call(
         kernel,
         out_shape=jax.ShapeDtypeStruct(source.shape, F32),
-        in_specs=[vmem, vmem, hbm, smem, hbm, smem, smem, hbm, smem, smem],
+        in_specs=[vmem, vmem, vmem, smem, vmem, smem, smem, vmem, smem, smem],
         out_specs=vmem,
         scratch_shapes=[
-            pltpu.VMEM(diag.shape, F32),
-            pltpu.VMEM(local.shape, BF16),
-            pltpu.VMEM(send.shape[2:], BF16),
+            pltpu.VMEM(send.shape, F32),
             pltpu.VMEM((elements, 2 * W, W), F32),
             pltpu.VMEM((elements, 2 * W, 2 * W), BF16),
             pltpu.VMEM((elements, W, 6 * W), BF16),
             pltpu.VMEM((4, slots, W, 2 * W), BF16),
             pltpu.VMEM((SWEEPS, 8, 8, W), F32),
             pltpu.VMEM((SWEEPS, 8, 8, W), F32),
-            pltpu.SemaphoreType.DMA((3,)),
             pltpu.SemaphoreType.DMA((SWEEPS, 8)),
             pltpu.SemaphoreType.DMA((SWEEPS, 8)),
         ],
         compiler_params=pltpu.CompilerParams(
             collective_id=0, has_side_effects=True, vmem_limit_bytes=48 * 1024 * 1024
         ),
-    )(*args)
+    )(source, prev, diag, near, local, send_el, count, send, recv_el, layers)
 
 
 def solution(mesh):

time: 31.6 us -> 27.6 us (0.87)
  local copies, waits for them, and re-layouts: 6.54 us -> 2.87 us
    unnamed x17 -> x20, local copies, waits for them, and re-layouts: 6.54 us -> 2.87 us
where the time goes in v1:
time: 27.6 us; the launch traced here: 27.5 us
  Pallas kernels  24.4 us (88%)
  local copies, waits for them, and re-layouts  2.87 us (10%)
    pallas_call x1, Pallas kernels, on_device(): pl.pallas_call(kernel, out_shape=jax.ShapeDtypeStruct(source.shape, F32),...  24.4 us
    unnamed x20, local copies, waits for them, and re-layouts  2.87 us

profile of v1, /device:TPU:1, one launch (start us, length us, event | category | flops | bytes accessed | tf_op | source)
XLA Modules:
  0.0 27.5 jit_solution(2590117600972920289)
XLA Ops:
  0.0 0.0 copy-start.8
  0.0 0.0 copy-start.6
  0.0 0.0 copy-start.1
  0.0 0.0 copy-start.7
  0.0 0.0 copy-start.5
  0.0 0.0 copy-start.4
  0.0 0.0 copy-start
  0.0 0.0 copy-start.3
  0.1 0.0 copy-start.2
  0.1 2.2 %copy.11.local_in = bf16[16,4,125,125]{3,2,1,0:T(8,128)(2,1)S(1)} copy(bf16[16,4,125,125]{3,1,2,0:T(4,128)(2,1)} %param.14) | data formatting | bytes 4000000 | tf_op args[4]
  2.3 0.0 copy-done.8
  2.3 0.0 copy-done.6
  2.3 0.0 copy-done.1
  2.3 0.0 copy-done.7
  2.4 0.0 copy-done.5
  2.4 0.0 copy-done.4
  2.4 0.0 copy-done
  2.4 0.0 copy-done.3
  2.4 0.0 copy-done.2
  2.4 24.4 %shard_map.100 = f32[16,125]{1,0:T(8,128)S(1)} custom-call(f32[16,125]{1,0:T(8,128)S(1)} %copy-done.2, f32[16,125]{1,0:T(8,128)S(1)} %copy-done.3, f32[2000,125]{1,0:T(8,128)S(1)} %bitcast.15, s32[4,16]{1,0:T(4,128)S(1)} %bitcast.17, bf16[16,4,125,125]{3,2,1,0:T(8,128)(2,1)S(1)} %copy.11.local_in, s32[3,1,8]{2,1,0:T(1,128)S(1)} %bitcast.18, ...), custom_call_target="tpu_custom_call" | custom-call | tf_op jit(solution)/shard_map/pallas_call | solution.py:279
  26.9 0.6 %copy.13 = f32[16,125]{1,0:T(8,128)} copy(f32[16,125]{1,0:T(8,128)S(1)} %shard_map.100) | data formatting | bytes 16000
Async XLA Ops:
  0.0 2.3 %copy-start.8 = (s32[4]{0:T(128)S(1)}, s32[4]{0:T(128)}, u32[]{:S(2)}) copy-start(s32[4]{0:T(128)} %layer_ref.1) | copy-start | bytes 52
  0.0 2.3 %copy-start.6 = (s32[1,1,8,3]{2,1,3,0:T(1,128)S(1)}, s32[1,1,8,3]{2,1,3,0:T(1,128)}, u32[]{:S(2)}) copy-start(s32[1,1,8,3]{2,1,3,0:T(1,128)} %param.18) | copy-start | bytes 292
  0.0 2.3 %copy-start.1 = (bf16[1,1,8,3,125,125]{5,2,4,3,1,0:T(8,128)(2,1)S(1)}, bf16[1,1,8,3,125,125]{5,2,4,3,1,0:T(8,128)(2,1)}, u32[]{:S(2)}) copy-start(bf16[1,1,8,3,125,125]{5,2,4,3,1,0:T(8,128)(2,1)} %param.17) | copy-start | bytes 2250004
  0.0 2.3 %copy-start.7 = (s32[1,1,8]{2,1,0:T(1,128)S(1)}, s32[1,1,8]{2,1,0:T(1,128)}, u32[]{:S(2)}) copy-start(s32[1,1,8]{2,1,0:T(1,128)} %count_ref.1) | copy-start | bytes 100
  0.0 2.3 %copy-start.5 = (s32[1,1,8,3]{2,1,3,0:T(1,128)S(1)}, s32[1,1,8,3]{2,1,3,0:T(1,128)}, u32[]{:S(2)}) copy-start(s32[1,1,8,3]{2,1,3,0:T(1,128)} %param.15) | copy-start | bytes 292
  0.0 2.3 %copy-start.4 = (s32[16,4]{0,1:T(4,128)S(1)}, s32[16,4]{0,1:T(4,128)}, u32[]{:S(2)}) copy-start(s32[16,4]{0,1:T(4,128)} %param.13) | copy-start | bytes 772
  0.0 2.3 %copy-start = (f32[16,125,125]{2,0,1:T(8,128)S(1)}, f32[16,125,125]{2,0,1:T(8,128)}, u32[]{:S(2)}) copy-start(f32[16,125,125]{2,0,1:T(8,128)} %param.12) | copy-start | bytes 3000004
  0.0 2.3 %copy-start.3 = (f32[16,125]{1,0:T(8,128)S(1)}, f32[16,125]{1,0:T(8,128)}, u32[]{:S(2)}) copy-start(f32[16,125]{1,0:T(8,128)} %prev_ref.1) | copy-start | bytes 24004
  0.1 2.3 %copy-start.2 = (f32[16,125]{1,0:T(8,128)S(1)}, f32[16,125]{1,0:T(8,128)}, u32[]{:S(2)}) copy-start(f32[16,125]{1,0:T(8,128)} %source_ref.1) | copy-start | bytes 24004

commit v2 on v1

--- a/solution.py
+++ b/solution.py
@@ -12,6 +12,8 @@
 SWEEPS = 3
 RELAXATION = 0.8
 OFFSETS = ((-1, -1), (-1, 0), (-1, 1), (0, -1), (0, 1), (1, -1), (1, 0), (1, 1))
+FAR_FIRST = (0, 2, 5, 7, 1, 6, 3, 4)
+ROWS = 4
 MESH = pl.DeviceIdType.MESH
 BF16 = jnp.bfloat16
 F32 = jnp.float32
@@ -46,6 +48,7 @@
     layer_ref,
     out_ref,
     send_wide,
+    local_wide,
     fx_f,
     fx_s,
     blocks,
@@ -79,7 +82,7 @@
         @pl.when(jnp.logical_not(exists))
         def _():
             for t in range(SWEEPS):
-                recvbuf[t, k] = jnp.zeros((8, W), F32)
+                recvbuf[t, k] = jnp.zeros((ROWS, W), F32)
 
     lane = lax.broadcasted_iota(jnp.int32, (W, W), 1)
     lane_row = lax.broadcasted_iota(jnp.int32, (1, W), 1)
@@ -94,17 +97,14 @@
         count = count_ref[0, 0, k]
         for s in range(slots):
             chosen = jnp.where(s < count, send_el_ref[s, 0, k], -1)
-            index = jnp.where(lane_row == 64 + 8 * k + s, chosen, index)
+            index = jnp.where(lane_row == 64 + ROWS * k + s, chosen, index)
     select = (lax.broadcasted_iota(jnp.int32, (W, W), 0) == index).astype(F32).astype(BF16)
-    row8 = lax.broadcasted_iota(jnp.int32, (8, W), 0)
-    scatter_rows = []
+    row = lax.broadcasted_iota(jnp.int32, (8 * ROWS, W), 0)
+    scatter = jnp.full((8 * ROWS, W), -1, jnp.int32)
     for k in range(8):
-        target_el = jnp.full((8, W), -1, jnp.int32)
         for s in range(slots):
-            target_el = jnp.where(row8 == s, recv_el_ref[s, 0, k], target_el)
-        scatter_rows.append(target_el)
-    scatter = jnp.concatenate(scatter_rows, axis=0)
-    scatter = (scatter == lax.broadcasted_iota(jnp.int32, (64, W), 1) % GROUP).astype(F32).astype(BF16)
+            scatter = jnp.where(row == ROWS * k + s, recv_el_ref[s, 0, k], scatter)
+    scatter = (scatter == lax.broadcasted_iota(jnp.int32, (8 * ROWS, W), 1) % GROUP).astype(F32).astype(BF16)
 
     depth = jnp.zeros((1, W), jnp.int32)
     for c in range(elements // LAYERS):
@@ -123,16 +123,18 @@
 
     def send_part(t, g):
         zero = jnp.zeros_like(g)
-        low = jnp.where((lane >= 64) & (lane < 96), g, zero)
-        high = jnp.where(lane >= 96, g, zero)
+        low = jnp.where((lane >= 64) & (lane < 64 + 4 * ROWS), g, zero)
+        high = jnp.where(lane >= 64 + 4 * ROWS, g, zero)
         rhs = jnp.concatenate([low, high], axis=0).astype(BF16)
         acc = zero
         for k in range(4):
             res = dot(sends[k].reshape(slots * W, 2 * W), rhs)
             for s in range(slots):
-                acc = jnp.where((lane >= 64) & (lane % 32 == 8 * k + s), res[s * W : (s + 1) * W], acc)
-        sendbuf[t] = acc.T[64:].reshape(8, 8, W)
+                acc = jnp.where((lane >= 64) & (lane < 64 + 8 * ROWS) & (lane % (4 * ROWS) == ROWS * k + s), res[s * W : (s + 1) * W], acc)
+        outgoing = acc.T
         for k in range(8):
+            sendbuf[t, k] = outgoing[64 + ROWS * k : 64 + ROWS * (k + 1)]
+        for k in FAR_FIRST:
             exists, target = there(k)
 
             @pl.when(exists)
@@ -149,17 +151,6 @@
             device_id_type=MESH,
         )
 
-    send_wide[...] = send_in[...].astype(F32)
-    for k in range(4):
-        for s in range(slots):
-            for half in range(2):
-                rows = pl.ds(s * width * 8 + k + 4 * half, width, stride=8)
-                block = padded(send_wide[rows, :], W).astype(BF16)
-                sends[k, s, :, half * W : (half + 1) * W] = block
-    pl.semaphore_wait(barrier, present)
-    g = gathered(pressure)
-    send_part(0, g)
-
     def doubled(x):
         return jnp.concatenate([x, x], axis=0)
 
@@ -170,8 +161,8 @@
         fx_s[e, start : start + rows, W : 2 * W] = lo
 
     def prepare_diag(i, carry):
-        for u in range(CHUNK):
-            e = i * CHUNK + u
+        for u in range(2 * CHUNK):
+            e = i * 2 * CHUNK + u
             m = padded(diag_in[pl.ds(e, width, stride=elements), :], W)
             magnitude = jnp.abs(m)
             column_norm = jnp.max(jnp.sum(magnitude, axis=0, keepdims=True), axis=1, keepdims=True)
@@ -188,7 +179,7 @@
             store_split(e, 0, f)
         return carry
 
-    lax.fori_loop(0, elements // CHUNK, prepare_diag, 0)
+    lax.fori_loop(0, elements // (2 * CHUNK), prepare_diag, 0)
 
     def step(k, carry):
         for e in range(elements):
@@ -199,17 +190,33 @@
             store_split(e, 0, new)
         return carry
 
-    lax.fori_loop(0, NS_ITERS - 1, step, 0)
+    def prepare_local(k, carry):
+        rows = CHUNK * width * faces
+        local_wide[...] = local_in[pl.ds(pl.multiple_of(k * rows, 16), rows), :].astype(F32)
+        for u in range(CHUNK):
+            for f in range(faces):
+                block = local_wide[pl.ds(u * width * faces + f, width, stride=faces), :]
+                blocks[k * CHUNK + u, :, f * W : (f + 1) * W] = padded(block, W).astype(BF16)
+        return step(k, carry)
+
+    send_wide[...] = send_in[...].astype(F32)
+    for k in range(4):
+        for s in range(slots):
+            for half in range(2):
+                rows = pl.ds(s * width * 8 + k + 4 * half, width, stride=8)
+                block = padded(send_wide[rows, :], W).astype(BF16)
+                sends[k, s, :, half * W : (half + 1) * W] = block
+    step(0, 0)
+    pl.semaphore_wait(barrier, present)
+    g = gathered(pressure)
+    send_part(0, g)
+
+    chunks = elements // CHUNK
+    lax.fori_loop(0, chunks, prepare_local, 0)
+    lax.fori_loop(chunks, NS_ITERS - 2, step, 0)
     for e in range(elements):
         res = dot(fx_s[e, W:], doubled(fx_s[e, :W]))
         store_split(e, W, 2.0 * fx_f[e, W:] - (res[:, :W] + res[:, W:]))
-
-    def prepare_local(e, carry):
-        for f in range(faces):
-            blocks[e, :, f * W : (f + 1) * W] = padded(local_in[e, f], W)
-        return carry
-
-    lax.fori_loop(0, elements, prepare_local, 0)
 
     def per_element(load, rhs):
         acc = jnp.zeros((W, W), F32)
@@ -239,7 +246,7 @@
             def _():
                 remote(t, k, k, target).wait_recv()
 
-        arrived = recvbuf[t].reshape(64, W).T
+        arrived = jnp.concatenate([recvbuf[t, k] for k in range(8)], axis=0).T
         arrived_hi, arrived_lo = split(arrived)
         residual = local - (dot(arrived_hi, scatter) + dot(arrived_lo, scatter))
         hi, lo = split(residual)
@@ -271,6 +278,7 @@
     slots = send_el.shape[3]
     diag = diag.transpose(1, 0, 2).reshape(width * elements, width)
     send = send[0, 0].transpose(1, 2, 0, 3).reshape(slots * width * 8, width)
+    local = local.transpose(0, 2, 1, 3).reshape(elements * width * faces, width)
     near = near.T
     send_el = send_el.transpose(3, 0, 1, 2).reshape(slots, 1, 8)
     recv_el = recv_el.transpose(3, 0, 1, 2).reshape(slots, 1, 8)
@@ -283,12 +291,13 @@
         out_specs=vmem,
         scratch_shapes=[
             pltpu.VMEM(send.shape, F32),
+            pltpu.VMEM((CHUNK * width * faces, width), F32),
             pltpu.VMEM((elements, 2 * W, W), F32),
             pltpu.VMEM((elements, 2 * W, 2 * W), BF16),
             pltpu.VMEM((elements, W, 6 * W), BF16),
             pltpu.VMEM((4, slots, W, 2 * W), BF16),
-            pltpu.VMEM((SWEEPS, 8, 8, W), F32),
-            pltpu.VMEM((SWEEPS, 8, 8, W), F32),
+            pltpu.VMEM((SWEEPS, 8, ROWS, W), F32),
+            pltpu.VMEM((SWEEPS, 8, ROWS, W), F32),
             pltpu.SemaphoreType.DMA((SWEEPS, 8)),
             pltpu.SemaphoreType.DMA((SWEEPS, 8)),
         ],

time: 27.6 us -> 32.5 us (1.18)
  local copies, waits for them, and re-layouts: 2.87 us -> 9.26 us
  Pallas kernels: 24.4 us -> 22.9 us
    unnamed x20 -> x21, local copies, waits for them, and re-layouts: 2.87 us -> 9.26 us
    pallas_call x1, Pallas kernels: 24.4 us -> 22.9 us  [on_device(): pl.pallas_call(kernel, out_shape=jax.ShapeDtypeStruct(source.shape, F32),...]
where the time goes in v2:
time: 32.5 us; the launch traced here: 32.1 us
  Pallas kernels  22.9 us (70%)
  local copies, waits for them, and re-layouts  9.26 us (28%)
    pallas_call x1, Pallas kernels, on_device(): pl.pallas_call(kernel, out_shape=jax.ShapeDtypeStruct(source.shape, F32),...  22.9 us
    unnamed x21, local copies, waits for them, and re-layouts  9.26 us

profile of v2, /device:TPU:1, one launch (start us, length us, event | category | flops | bytes accessed | tf_op | source)
XLA Modules:
  0.0 32.1 jit_solution(12433745779254731641)
XLA Ops:
  0.0 0.0 copy-start
  0.0 1.6 %copy-done = bf16[16,4,125,125]{3,1,2,0:T(4,128)(2,1)S(1)} copy-done((bf16[16,4,125,125]{3,1,2,0:T(4,128)(2,1)S(1)}, bf16[16,4,125,125]{3,1,2,0:T(4,128)(2,1)}, u32[]{:S(2)}) %copy-start) | copy-done | bytes 2000024
  1.6 0.0 copy-start.1
  1.6 1.2 %copy-done.1 = f32[16,125,125]{2,0,1:T(8,128)S(1)} copy-done((f32[16,125,125]{2,0,1:T(8,128)S(1)}, f32[16,125,125]{2,0,1:T(8,128)}, u32[]{:S(2)}) %copy-start.1) | copy-done | bytes 1000024
  2.8 0.0 copy-start.2
  2.8 1.1 %copy-done.2 = bf16[1,1,8,3,125,125]{5,2,4,3,1,0:T(8,128)(2,1)S(1)} copy-done((bf16[1,1,8,3,125,125]{5,2,4,3,1,0:T(8,128)(2,1)S(1)}, bf16[1,1,8,3,125,125]{5,2,4,3,1,0:T(8,128)(2,1)}, u32[]{:S(2)}) %copy-start.2) | copy-done | bytes 750024
  3.9 0.0 copy-start.3
  3.9 0.7 %copy-done.3 = f32[16,125]{1,0:T(8,128)S(1)} copy-done((f32[16,125]{1,0:T(8,128)S(1)}, f32[16,125]{1,0:T(8,128)}, u32[]{:S(2)}) %copy-start.3) | copy-done | bytes 8024
  4.6 0.0 copy-start.4
  4.6 0.7 %copy-done.4 = f32[16,125]{1,0:T(8,128)S(1)} copy-done((f32[16,125]{1,0:T(8,128)S(1)}, f32[16,125]{1,0:T(8,128)}, u32[]{:S(2)}) %copy-start.4) | copy-done | bytes 8024
  5.3 0.0 copy-start.5
  5.3 0.7 %copy-done.5 = s32[16,4]{0,1:T(4,128)S(1)} copy-done((s32[16,4]{0,1:T(4,128)S(1)}, s32[16,4]{0,1:T(4,128)}, u32[]{:S(2)}) %copy-start.5) | copy-done | bytes 280
  6.0 0.0 copy-start.6
  6.0 0.7 %copy-done.6 = s32[1,1,8,3]{2,1,3,0:T(1,128)S(1)} copy-done((s32[1,1,8,3]{2,1,3,0:T(1,128)S(1)}, s32[1,1,8,3]{2,1,3,0:T(1,128)}, u32[]{:S(2)}) %copy-start.6) | copy-done | bytes 120
  6.7 0.0 copy-start.7
  6.7 0.7 %copy-done.7 = s32[1,1,8,3]{2,1,3,0:T(1,128)S(1)} copy-done((s32[1,1,8,3]{2,1,3,0:T(1,128)S(1)}, s32[1,1,8,3]{2,1,3,0:T(1,128)}, u32[]{:S(2)}) %copy-start.7) | copy-done | bytes 120
  7.4 0.0 copy-start.8
  7.4 0.7 %copy-done.8 = s32[1,1,8]{2,1,0:T(1,128)S(1)} copy-done((s32[1,1,8]{2,1,0:T(1,128)S(1)}, s32[1,1,8]{2,1,0:T(1,128)}, u32[]{:S(2)}) %copy-start.8) | copy-done | bytes 56
  8.0 0.0 copy-start.9
  8.0 0.7 %copy-done.9 = s32[4]{0:T(128)S(1)} copy-done((s32[4]{0:T(128)S(1)}, s32[4]{0:T(128)}, u32[]{:S(2)}) %copy-start.9) | copy-done | bytes 40
  8.7 22.9 %shard_map.100 = f32[16,125]{1,0:T(8,128)S(1)} custom-call(f32[16,125]{1,0:T(8,128)S(1)} %copy-done.3, f32[16,125]{1,0:T(8,128)S(1)} %copy-done.4, f32[2000,125]{1,0:T(8,128)S(1)} %bitcast.19, s32[4,16]{1,0:T(4,128)S(1)} %bitcast.21, bf16[8000,125]{1,0:T(8,128)(2,1)S(1)} %bitcast.18, s32[3,1,8]{2,1,0:T(1,128)S(1)} %bitcast.22, s32[1,1,8]{2,1,0:T(1,128)S(1)} %copy-done.8, ...), custom_call_target="tpu_custom_call" | custom-call | tf_op jit(solution)/shard_map/pallas_call | solution.py:287
  31.5 0.6 %copy.12 = f32[16,125]{1,0:T(8,128)} copy(f32[16,125]{1,0:T(8,128)S(1)} %shard_map.100) | data formatting | bytes 16000
Async XLA Ops:
  0.0 1.6 %copy-start = (bf16[16,4,125,125]{3,1,2,0:T(4,128)(2,1)S(1)}, bf16[16,4,125,125]{3,1,2,0:T(4,128)(2,1)}, u32[]{:S(2)}) copy-start(bf16[16,4,125,125]{3,1,2,0:T(4,128)(2,1)} %param.14) | copy-start | bytes 6000004
  1.6 1.2 %copy-start.1 = (f32[16,125,125]{2,0,1:T(8,128)S(1)}, f32[16,125,125]{2,0,1:T(8,128)}, u32[]{:S(2)}) copy-start(f32[16,125,125]{2,0,1:T(8,128)} %param.12) | copy-start | bytes 3000004
  2.8 1.1 %copy-start.2 = (bf16[1,1,8,3,125,125]{5,2,4,3,1,0:T(8,128)(2,1)S(1)}, bf16[1,1,8,3,125,125]{5,2,4,3,1,0:T(8,128)(2,1)}, u32[]{:S(2)}) copy-start(bf16[1,1,8,3,125,125]{5,2,4,3,1,0:T(8,128)(2,1)} %param.17) | copy-start | bytes 2250004
  3.9 0.7 %copy-start.3 = (f32[16,125]{1,0:T(8,128)S(1)}, f32[16,125]{1,0:T(8,128)}, u32[]{:S(2)}) copy-start(f32[16,125]{1,0:T(8,128)} %source_ref.1) | copy-start | bytes 24004
  4.6 0.7 %copy-start.4 = (f32[16,125]{1,0:T(8,128)S(1)}, f32[16,125]{1,0:T(8,128)}, u32[]{:S(2)}) copy-start(f32[16,125]{1,0:T(8,128)} %prev_ref.1) | copy-start | bytes 24004
  5.3 0.7 %copy-start.5 = (s32[16,4]{0,1:T(4,128)S(1)}, s32[16,4]{0,1:T(4,128)}, u32[]{:S(2)}) copy-start(s32[16,4]{0,1:T(4,128)} %param.13) | copy-start | bytes 772
  6.0 0.7 %copy-start.6 = (s32[1,1,8,3]{2,1,3,0:T(1,128)S(1)}, s32[1,1,8,3]{2,1,3,0:T(1,128)}, u32[]{:S(2)}) copy-start(s32[1,1,8,3]{2,1,3,0:T(1,128)} %param.15) | copy-start | bytes 292
  6.7 0.7 %copy-start.7 = (s32[1,1,8,3]{2,1,3,0:T(1,128)S(1)}, s32[1,1,8,3]{2,1,3,0:T(1,128)}, u32[]{:S(2)}) copy-start(s32[1,1,8,3]{2,1,3,0:T(1,128)} %param.18) | copy-start | bytes 292
  7.4 0.7 %copy-start.8 = (s32[1,1,8]{2,1,0:T(1,128)S(1)}, s32[1,1,8]{2,1,0:T(1,128)}, u32[]{:S(2)}) copy-start(s32[1,1,8]{2,1,0:T(1,128)} %count_ref.1) | copy-start | bytes 100
  8.0 0.7 %copy-start.9 = (s32[4]{0:T(128)S(1)}, s32[4]{0:T(128)}, u32[]{:S(2)}) copy-start(s32[4]{0:T(128)} %layer_ref.1) | copy-start | bytes 52

commit v3 on v2

--- a/solution.py
+++ b/solution.py
@@ -48,7 +48,6 @@
     layer_ref,
     out_ref,
     send_wide,
-    local_wide,
     fx_f,
     fx_s,
     blocks,
@@ -190,14 +189,10 @@
             store_split(e, 0, new)
         return carry
 
-    def prepare_local(k, carry):
-        rows = CHUNK * width * faces
-        local_wide[...] = local_in[pl.ds(pl.multiple_of(k * rows, 16), rows), :].astype(F32)
-        for u in range(CHUNK):
-            for f in range(faces):
-                block = local_wide[pl.ds(u * width * faces + f, width, stride=faces), :]
-                blocks[k * CHUNK + u, :, f * W : (f + 1) * W] = padded(block, W).astype(BF16)
-        return step(k, carry)
+    def prepare_local(e, carry):
+        for f in range(faces):
+            blocks[e, :, f * W : (f + 1) * W] = padded(local_in[e, f], W)
+        return carry
 
     send_wide[...] = send_in[...].astype(F32)
     for k in range(4):
@@ -211,9 +206,8 @@
     g = gathered(pressure)
     send_part(0, g)
 
-    chunks = elements // CHUNK
-    lax.fori_loop(0, chunks, prepare_local, 0)
-    lax.fori_loop(chunks, NS_ITERS - 2, step, 0)
+    lax.fori_loop(0, elements, prepare_local, 0)
+    lax.fori_loop(1, NS_ITERS - 1, step, 0)
     for e in range(elements):
         res = dot(fx_s[e, W:], doubled(fx_s[e, :W]))
         store_split(e, W, 2.0 * fx_f[e, W:] - (res[:, :W] + res[:, W:]))
@@ -278,7 +272,6 @@
     slots = send_el.shape[3]
     diag = diag.transpose(1, 0, 2).reshape(width * elements, width)
     send = send[0, 0].transpose(1, 2, 0, 3).reshape(slots * width * 8, width)
-    local = local.transpose(0, 2, 1, 3).reshape(elements * width * faces, width)
     near = near.T
     send_el = send_el.transpose(3, 0, 1, 2).reshape(slots, 1, 8)
     recv_el = recv_el.transpose(3, 0, 1, 2).reshape(slots, 1, 8)
@@ -291,7 +284,6 @@
         out_specs=vmem,
         scratch_shapes=[
             pltpu.VMEM(send.shape, F32),
-            pltpu.VMEM((CHUNK * width * faces, width), F32),
             pltpu.VMEM((elements, 2 * W, W), F32),
             pltpu.VMEM((elements, 2 * W, 2 * W), BF16),
             pltpu.VMEM((elements, W, 6 * W), BF16),

time: 32.5 us -> 25.6 us (0.79)
  local copies, waits for them, and re-layouts: 9.26 us -> 2.87 us
  Pallas kernels: 22.9 us -> 22.4 us
    unnamed x21 -> x20, local copies, waits for them, and re-layouts: 9.26 us -> 2.87 us
    pallas_call x1, Pallas kernels: 22.9 us -> 22.4 us  [on_device(): pl.pallas_call(kernel, out_shape=jax.ShapeDtypeStruct(source.shape, F32),...]
where the time goes in v3:
time: 25.6 us; the launch traced here: 25.4 us
  Pallas kernels  22.4 us (88%)
  local copies, waits for them, and re-layouts  2.87 us (11%)
    pallas_call x1, Pallas kernels, on_device(): pl.pallas_call(kernel, out_shape=jax.ShapeDtypeStruct(source.shape, F32),...  22.4 us
    unnamed x20, local copies, waits for them, and re-layouts  2.87 us

profile of v3, /device:TPU:1, one launch (start us, length us, event | category | flops | bytes accessed | tf_op | source)
XLA Modules:
  0.0 25.4 jit_solution(7295401183206633530)
XLA Ops:
  0.0 0.0 copy-start.8
  0.0 0.0 copy-start.6
  0.0 0.0 copy-start.1
  0.0 0.0 copy-start.7
  0.0 0.0 copy-start.5
  0.0 0.0 copy-start.4
  0.0 0.0 copy-start
  0.0 0.0 copy-start.3
  0.1 0.0 copy-start.2
  0.1 2.2 %copy.11.local_in = bf16[16,4,125,125]{3,2,1,0:T(8,128)(2,1)S(1)} copy(bf16[16,4,125,125]{3,1,2,0:T(4,128)(2,1)} %param.14) | data formatting | bytes 4000000 | tf_op args[4]
  2.3 0.0 copy-done.8
  2.3 0.0 copy-done.6
  2.3 0.0 copy-done.1
  2.3 0.0 copy-done.7
  2.4 0.0 copy-done.5
  2.4 0.0 copy-done.4
  2.4 0.0 copy-done
  2.4 0.0 copy-done.3
  2.4 0.0 copy-done.2
  2.4 22.4 %shard_map.100 = f32[16,125]{1,0:T(8,128)S(1)} custom-call(f32[16,125]{1,0:T(8,128)S(1)} %copy-done.2, f32[16,125]{1,0:T(8,128)S(1)} %copy-done.3, f32[2000,125]{1,0:T(8,128)S(1)} %bitcast.15, s32[4,16]{1,0:T(4,128)S(1)} %bitcast.17, bf16[16,4,125,125]{3,2,1,0:T(8,128)(2,1)S(1)} %copy.11.local_in, s32[3,1,8]{2,1,0:T(1,128)S(1)} %bitcast.18, ...), custom_call_target="tpu_custom_call" | custom-call | tf_op jit(solution)/shard_map/pallas_call | solution.py:280
  24.8 0.6 %copy.13 = f32[16,125]{1,0:T(8,128)} copy(f32[16,125]{1,0:T(8,128)S(1)} %shard_map.100) | data formatting | bytes 16000
Async XLA Ops:
  0.0 2.3 %copy-start.8 = (s32[4]{0:T(128)S(1)}, s32[4]{0:T(128)}, u32[]{:S(2)}) copy-start(s32[4]{0:T(128)} %layer_ref.1) | copy-start | bytes 52
  0.0 2.3 %copy-start.6 = (s32[1,1,8,3]{2,1,3,0:T(1,128)S(1)}, s32[1,1,8,3]{2,1,3,0:T(1,128)}, u32[]{:S(2)}) copy-start(s32[1,1,8,3]{2,1,3,0:T(1,128)} %param.18) | copy-start | bytes 292
  0.0 2.3 %copy-start.1 = (bf16[1,1,8,3,125,125]{5,2,4,3,1,0:T(8,128)(2,1)S(1)}, bf16[1,1,8,3,125,125]{5,2,4,3,1,0:T(8,128)(2,1)}, u32[]{:S(2)}) copy-start(bf16[1,1,8,3,125,125]{5,2,4,3,1,0:T(8,128)(2,1)} %param.17) | copy-start | bytes 2250004
  0.0 2.3 %copy-start.7 = (s32[1,1,8]{2,1,0:T(1,128)S(1)}, s32[1,1,8]{2,1,0:T(1,128)}, u32[]{:S(2)}) copy-start(s32[1,1,8]{2,1,0:T(1,128)} %count_ref.1) | copy-start | bytes 100
  0.0 2.3 %copy-start.5 = (s32[1,1,8,3]{2,1,3,0:T(1,128)S(1)}, s32[1,1,8,3]{2,1,3,0:T(1,128)}, u32[]{:S(2)}) copy-start(s32[1,1,8,3]{2,1,3,0:T(1,128)} %param.15) | copy-start | bytes 292
  0.0 2.3 %copy-start.4 = (s32[16,4]{0,1:T(4,128)S(1)}, s32[16,4]{0,1:T(4,128)}, u32[]{:S(2)}) copy-start(s32[16,4]{0,1:T(4,128)} %param.13) | copy-start | bytes 772
  0.0 2.3 %copy-start = (f32[16,125,125]{2,0,1:T(8,128)S(1)}, f32[16,125,125]{2,0,1:T(8,128)}, u32[]{:S(2)}) copy-start(f32[16,125,125]{2,0,1:T(8,128)} %param.12) | copy-start | bytes 3000004
  0.0 2.3 %copy-start.3 = (f32[16,125]{1,0:T(8,128)S(1)}, f32[16,125]{1,0:T(8,128)}, u32[]{:S(2)}) copy-start(f32[16,125]{1,0:T(8,128)} %prev_ref.1) | copy-start | bytes 24004
  0.1 2.3 %copy-start.2 = (f32[16,125]{1,0:T(8,128)S(1)}, f32[16,125]{1,0:T(8,128)}, u32[]{:S(2)}) copy-start(f32[16,125]{1,0:T(8,128)} %source_ref.1) | copy-start | bytes 24004
